TPU v7x, 32 devices: a whole 2x2x4 slice. The times are simulated.
32 devices in a mesh: groups: 2 (over y), gy: 4 (over z), gx: 2 (over x), gz: 2 (over core).
Axes of the slice: x: 2, y: 2, z: 4, core: 2. Of those that a mesh axis runs over, the one named last changes fastest.
Arguments:
- charge_density: float32 [32, 32, 256], P(('groups', 'gx'), 'gy', 'gz'), parts along dimension 0, may hold values from -8 to 8
- permittivity: float32 [32, 32, 256], P(('groups', 'gx'), 'gy', 'gz'), parts along dimension 0, may hold values from 1 to 78
- ion_centers: float32 [4, 4, 2, 3, 4, 8], P(('groups', 'gx'), 'gy', 'gz'), parts along dimension 0, may hold values from -1 to 9
- ion_widths: float32 [4, 4, 2, 4, 8], P(('groups', 'gx'), 'gy', 'gz'), parts along dimension 0, may hold values from 1 to 2.5
- ion_charges: float32 [4, 4, 2, 4, 8], P(('groups', 'gx'), 'gy', 'gz'), parts along dimension 0, may hold values from -8 to 8
- block_counts: int32 [4, 4, 2, 4], P(('groups', 'gx'), 'gy', 'gz'), parts along dimension 0, may hold values from 0 to 8, as said below
- block_anchors: int32 [4, 4, 2, 3, 4, 8], P(('groups', 'gx'), 'gy', 'gz'), parts along dimension 0, may hold values from 0 to 120, as said below
Outputs:
- potential: float32 [32, 32, 256], P(('groups', 'gx'), 'gy', 'gz'), parts along dimension 0
There are 2 independent parts, one for each index of `groups`. A program takes and returns all parts, laid end to end along the dimension named above; each array names one. Nothing has to cross between parts.
Inputs may be any that keep to these rules, and one draw needn't show every extreme that they name: `block_counts`: some brick rows, at least one, receive 8 live entries from every brick; the others fewer. `block_anchors`: component 0 lies in 0 to 0, component 1 in 0 to 0, component 2 in 0 to 120, so each block lies inside its brick.
All inputs are finite; a program needn't handle non-finite values.
Results may differ from a plain program's by a relative error of at most 0.0003.
Values may be sent and summed in bfloat16 or wider, within the bound.
A program may use at most 64 MiB of HBM per device.

v0:
```python
import math

import jax
import jax.numpy as jnp
from jax import lax
from jax.sharding import PartitionSpec as P

PATCH = 8
CAP = 8
LEVELS = 4
NU_PRE = 1
NU_POST = 1
NU_COARSE = 8


four_pi = 4.0 * math.pi
relax_weight = 2.0 / 3.0
gauss_norm = (2.0 * math.pi) ** 1.5


def padded_2(cells, sides, width):
    for axis, dim in sides:
        count = lax.axis_size(axis)
        ends = count - 1
        head = lax.slice_in_dim(cells, 0, width, axis=dim)
        tail = lax.slice_in_dim(cells, cells.shape[dim] - width, cells.shape[dim], axis=dim)
        cells = jnp.concatenate(
            [
                lax.ppermute(tail, axis, [(i, (i + 1) % count) for i in range(ends)]),
                cells,
                lax.ppermute(head, axis, [((i + 1) % count, i) for i in range(ends)]),
            ],
            axis=dim,
        )
    return cells


def gaussian_blocks(centre_x, centre_y, centre_z, spread, charge):
    positions = jnp.arange(PATCH, dtype=jnp.float32)
    decay_rate = 0.5 / (spread * spread)
    profile_x = jnp.exp(-((positions[None, :] - centre_x[:, None]) ** 2) * decay_rate[:, None])
    profile_y = jnp.exp(-((positions[None, :] - centre_y[:, None]) ** 2) * decay_rate[:, None])
    profile_z = jnp.exp(-((positions[None, :] - centre_z[:, None]) ** 2) * decay_rate[:, None])
    amplitude = charge / (gauss_norm * spread * spread * spread)
    blocks_out = (
        amplitude[:, None, None, None]
        * profile_x[:, :, None, None]
        * profile_y[:, None, :, None]
        * profile_z[:, None, None, :]
    )
    return blocks_out.reshape(centre_x.shape[0], PATCH * PATCH * PATCH)


def face_weights(padded):
    centre = padded[1:-1, 1:-1, 1:-1]
    weights = (
        0.5 * (centre + padded[2:, 1:-1, 1:-1]),
        0.5 * (centre + padded[:-2, 1:-1, 1:-1]),
        0.5 * (centre + padded[1:-1, 2:, 1:-1]),
        0.5 * (centre + padded[1:-1, :-2, 1:-1]),
        0.5 * (centre + padded[1:-1, 1:-1, 2:]),
        0.5 * (centre + padded[1:-1, 1:-1, :-2]),
    )
    weight_sum = weights[0] + weights[1] + weights[2] + weights[3] + weights[4] + weights[5]
    return (weights, weight_sum)


def apply_operator(padded, weights, weight_sum, spacing_factor):
    centre = padded[1:-1, 1:-1, 1:-1]
    beside = weights[0] * padded[2:, 1:-1, 1:-1] + weights[1] * padded[:-2, 1:-1, 1:-1]
    beside = beside + weights[2] * padded[1:-1, 2:, 1:-1] + weights[3] * padded[1:-1, :-2, 1:-1]
    beside = beside + weights[4] * padded[1:-1, 1:-1, 2:] + weights[5] * padded[1:-1, 1:-1, :-2]
    return spacing_factor * (weight_sum * centre - beside)


def restrict_mean(values):
    size_a, size_b, size_c = values.shape
    return values.reshape(size_a // 2, 2, size_b // 2, 2, size_c // 2, 2).mean(axis=(1, 3, 5))


def prolong(values):
    return jnp.repeat(jnp.repeat(jnp.repeat(values, 2, 0), 2, 1), 2, 2)


def halo_faces(values):
    return padded_2(values, (("gy", 1), ("gx", 0), ("gz", 2)), 1)


def halo_permittivity(values):
    return padded_2(values, (("gy", 1), ("gx", 0), ("gz", 2)), 1)


def smooth_sweeps(potential, source, weights, weight_sum, diagonal, spacing_factor, sweeps, padder):
    for sweep_index in range(sweeps):
        applied = apply_operator(padder(potential), weights, weight_sum, spacing_factor)
        potential = potential + relax_weight * (source - applied) / diagonal
    return potential


def coarse_solve(source, permittivity, spacing_factor, rim_padder, field_padder):
    weights, weight_sum = face_weights(rim_padder(permittivity))
    diagonal = spacing_factor * weight_sum
    potential = jnp.zeros_like(source)
    return smooth_sweeps(
        potential, source, weights, weight_sum, diagonal, spacing_factor, NU_COARSE, field_padder
    )


def multigrid_level(source, permittivity, level_index):
    spacing_factor = 1.0 / 4.0**level_index
    if level_index == LEVELS - 1:
        return coarse_solve(source, permittivity, spacing_factor, halo_permittivity, halo_faces)
    weights, weight_sum = face_weights(halo_permittivity(permittivity))
    diagonal = spacing_factor * weight_sum
    potential = jnp.zeros_like(source)
    potential = smooth_sweeps(
        potential, source, weights, weight_sum, diagonal, spacing_factor, NU_PRE, halo_faces
    )
    residual = source - apply_operator(halo_faces(potential), weights, weight_sum, spacing_factor)
    correction = multigrid_level(
        restrict_mean(residual), restrict_mean(permittivity), level_index + 1
    )
    potential = potential + prolong(correction)
    return smooth_sweeps(
        potential, source, weights, weight_sum, diagonal, spacing_factor, NU_POST, halo_faces
    )


def per_device(
    charge_density, permittivity, ion_centers, ion_widths, ion_charges, block_counts, block_anchors
):
    brick_rows = lax.axis_size("gy")
    cells_x, cells_y, cells_z = charge_density.shape
    slot_index = jnp.arange(CAP, dtype=jnp.int32)
    live_send = slot_index[None, :] < block_counts.reshape(brick_rows, 1)
    anchors = block_anchors.reshape(3, brick_rows, CAP)
    anchor_flat = (anchors[0] * cells_y + anchors[1]) * cells_z + anchors[2]
    anchor_flat = jnp.where(live_send, anchor_flat, -1)
    anchor_recv = lax.all_to_all(
        anchor_flat, "gy", split_axis=0, concat_axis=0, tiled=True
    ).reshape(-1)
    params = jnp.concatenate(
        [
            ion_centers.reshape(3, brick_rows, CAP),
            ion_widths.reshape(1, brick_rows, CAP),
            ion_charges.reshape(1, brick_rows, CAP),
        ],
        axis=0,
    )
    local_params = params.reshape(5, brick_rows * CAP)
    evaluated = gaussian_blocks(
        local_params[0], local_params[1], local_params[2], local_params[3], local_params[4]
    )
    outgoing = evaluated.astype(jnp.bfloat16).reshape(brick_rows, CAP, PATCH * PATCH * PATCH)
    arrived = lax.all_to_all(outgoing, "gy", split_axis=0, concat_axis=0, tiled=True)
    rounded = arrived.reshape(brick_rows * CAP, PATCH * PATCH * PATCH).astype(jnp.float32)
    live_recv = anchor_recv >= 0
    patch_steps = jnp.arange(PATCH, dtype=jnp.int32)
    offsets = (
        (patch_steps[:, None, None] * cells_y + patch_steps[None, :, None]) * cells_z
        + patch_steps[None, None, :]
    ).reshape(-1)
    targets = jnp.where(live_recv[:, None], anchor_recv[:, None] + offsets[None, :], 0)
    deposits = jnp.where(live_recv[:, None], rounded, 0.0)
    density = (
        charge_density.reshape(-1)
        .at[targets.reshape(-1)]
        .add(deposits.reshape(-1))
        .reshape(cells_x, cells_y, cells_z)
    )
    source = four_pi * density
    return multigrid_level(source, permittivity, 0)


def solution(mesh):
    placed = (
        P(("groups", "gx"), "gy", "gz"),
        P(("groups", "gx"), "gy", "gz"),
        P(("groups", "gx"), "gy", "gz", None, None, None),
        P(("groups", "gx"), "gy", "gz", None, None),
        P(("groups", "gx"), "gy", "gz", None, None),
        P(("groups", "gx"), "gy", "gz", None),
        P(("groups", "gx"), "gy", "gz", None, None, None),
    )
    return jax.shard_map(
        per_device,
        mesh=mesh,
        in_specs=placed,
        out_specs=P(("groups", "gx"), "gy", "gz"),
        check_vma=False,
    )
```

profile of v0, /device:TPU:0, one launch (start us, length us, event | category | flops | bytes accessed | tf_op | source)
XLA Modules:
  0.0 519.7 jit_solution(7458723773337971319)
XLA Ops:
  0.1 5.1 collective-permute-start.6
  10.2 4.5 collective-permute-start.54
  16.7 5.9 %all-to-all-start = ((s32[4,1,8]{2,1,0:T(1,128)}), s32[4,1,8]{2,1,0:T(1,128)S(1)}, u32[]{:S(2)}, u32[]{:S(2)}) async-start(s32[4,1,8]{2,1,0:T(1,128)} %bitcast.3), calls=%async_computation | async-start | bytes 4096 | tf_op jit(solution)/shard_map/all_to_all | solution.py:139
  22.6 3.9 collective-permute-start.60
  30.6 4.5 collective-permute-start.36
  36.5 4.5 collective-permute-start.57
  41.1 3.6 all-to-all-start.1
  47.7 4.6 collective-permute-start.42
  53.6 4.6 collective-permute-start.18
  59.5 4.5 collective-permute-start.39
  65.5 4.6 collective-permute-start.24
  71.4 4.6 collective-permute-start
  77.3 4.5 collective-permute-start.21
  88.7 4.5 collective-permute-start.3
  94.6 4.5 collective-permute-start.9
  100.6 3.0 collective-permute-start.5
  105.1 3.0 collective-permute-start.11
  108.2 113.4 %scatter_fusion = f32[8192]{0:T(1024)S(1)} fusion(f32[8192]{0:T(1024)S(1)} %bitcast.102, s32[16384]{0:T(1024)S(1)} %bitcast.105, f32[16384]{0:T(1024)S(1)} %broadcast_select_fusion), kind=kCustom, calls=%fused_computation | custom fusion | flops 16384 | bytes 262144 | tf_op jit(solution)/shard_map/scatter-add | solution.py:168
  224.4 3.8 collective-permute-start.12
  233.8 4.5 collective-permute-start.27
  239.7 4.5 collective-permute-start.15
  247.0 3.0 collective-permute-start.17
  261.3 4.2 collective-permute-start.45
  271.1 4.2 collective-permute-done.31
  276.6 4.5 collective-permute-start.33
  301.1 4.1 collective-permute-done.49
  306.5 4.5 collective-permute-start.51
  322.5 4.1 collective-permute-done.67
  328.0 4.5 collective-permute-start.69
  342.3 4.1 collective-permute-done.73
  347.8 4.5 collective-permute-start.75
  362.2 4.1 collective-permute-done.79
  367.6 4.5 collective-permute-start.81
  382.0 4.1 collective-permute-done.85
  387.4 4.5 collective-permute-start.87
  401.8 4.1 collective-permute-done.91
  407.2 4.5 collective-permute-start.93
  421.6 4.1 collective-permute-done.97
  427.1 4.5 collective-permute-start.99
  441.5 4.1 collective-permute-done.103
  446.9 4.5 collective-permute-start.105
  461.5 4.2 collective-permute-done.109
  466.9 4.5 collective-permute-start.111
  481.6 4.2 collective-permute-done.115
  487.1 4.5 collective-permute-start.117
  502.2 4.2 collective-permute-done.121
  507.7 4.5 collective-permute-start.123
  515.0 3.0 collective-permute-start.125
  (385 shorter events, 202.0 us)
Async XLA Ops:
  0.1 93.2 %collective-permute-start.6 = (f32[8,1,128]{2,1,0:T(1,128)S(1)}, f32[8,1,128]{2,1,0:T(1,128)S(1)}, u32[]{:S(2)}, u32[]{:S(2)}) collective-permute-start(f32[8,1,128]{2,1,0:T(1,128)S(1)} %broadcast.315), channel_id=1, source_target_pairs={{0,4},{4,8},{8,12},{1,5},{5,9},{9,13},{2,6},{6,10},{10,14},{3,7},{... | collective-permute-start | bytes 12296 | tf_op jit(solution)/shard_map/ppermute | solution.py:29
  5.1 88.1 %collective-permute-start.7 = (f32[8,1,128]{2,1,0:T(1,128)S(1)}, f32[8,1,128]{2,1,0:T(1,128)S(1)}, u32[]{:S(2)}, u32[]{:S(2)}) collective-permute-start(f32[8,1,128]{2,1,0:T(1,128)S(1)} %broadcast.315), channel_id=1, source_target_pairs={{4,0},{8,4},{12,8},{5,1},{9,5},{13,9},{6,2},{10,6},{14,10},{7,3},{... | collective-permute-start | bytes 12296 | tf_op jit(solution)/shard_map/ppermute | solution.py:31
  10.2 19.1 %collective-permute-start.54 = (f32[1,1,16]{2,1,0:T(1,128)S(1)}, f32[1,1,16]{2,1,0:T(1,128)S(1)}, u32[]{:S(2)}, u32[]{:S(2)}) collective-permute-start(f32[1,1,16]{2,1,0:T(1,128)S(1)} %multiply_bitcast_fusion), channel_id=1, source_target_pairs={{0,4},{4,8},{8,12},{1,5},{5,9},{9,13},{2,6},{6,10},{10,14},{3,7},{... | collective-permute-start | bytes 200 | tf_op jit(solution)/shard_map/ppermute | solution.py:29
  14.7 15.9 %collective-permute-start.55 = (f32[1,1,16]{2,1,0:T(1,128)S(1)}, f32[1,1,16]{2,1,0:T(1,128)S(1)}, u32[]{:S(2)}, u32[]{:S(2)}) collective-permute-start(f32[1,1,16]{2,1,0:T(1,128)S(1)} %multiply_bitcast_fusion), channel_id=1, source_target_pairs={{4,0},{8,4},{12,8},{5,1},{9,5},{13,9},{6,2},{10,6},{14,10},{7,3},{... | collective-permute-start | bytes 200 | tf_op jit(solution)/shard_map/ppermute | solution.py:31
  16.7 24.4 %all-to-all-start = ((s32[4,1,8]{2,1,0:T(1,128)}), s32[4,1,8]{2,1,0:T(1,128)S(1)}, u32[]{:S(2)}, u32[]{:S(2)}) async-start(s32[4,1,8]{2,1,0:T(1,128)} %bitcast.3), calls=%async_computation | async-start | bytes 4096 | tf_op jit(solution)/shard_map/all_to_all | solution.py:139
  22.6 12.6 %collective-permute-start.60 = (f32[1,1,16]{2,1,0:T(1,128)S(1)}, f32[1,1,16]{2,1,0:T(1,128)S(1)}, u32[]{:S(2)}, u32[]{:S(2)}) collective-permute-start(f32[1,1,16]{2,1,0:T(1,128)S(1)} %broadcast.329), channel_id=1, source_target_pairs={{0,4},{4,8},{8,12},{1,5},{5,9},{9,13},{2,6},{6,10},{10,14},{3,7},{... | collective-permute-start | bytes 200 | tf_op jit(solution)/shard_map/ppermute | solution.py:29
  29.3 7.2 %collective-permute-start.61 = (f32[1,1,16]{2,1,0:T(1,128)S(1)}, f32[1,1,16]{2,1,0:T(1,128)S(1)}, u32[]{:S(2)}, u32[]{:S(2)}) collective-permute-start(f32[1,1,16]{2,1,0:T(1,128)S(1)} %broadcast.329), channel_id=1, source_target_pairs={{4,0},{8,4},{12,8},{5,1},{9,5},{13,9},{6,2},{10,6},{14,10},{7,3},{... | collective-permute-start | bytes 200 | tf_op jit(solution)/shard_map/ppermute | solution.py:31
  30.6 21.7 %collective-permute-start.36 = (f32[2,1,32]{2,1,0:T(1,128)S(1)}, f32[2,1,32]{2,1,0:T(1,128)S(1)}, u32[]{:S(2)}, u32[]{:S(2)}) collective-permute-start(f32[2,1,32]{2,1,0:T(1,128)S(1)} %get-tuple-element.107), channel_id=1, source_target_pairs={{0,4},{4,8},{8,12},{1,5},{5,9},{9,13},{2,6},{6,10},{10,14},{3,7},{... | collective-permute-start | bytes 776 | tf_op jit(solution)/shard_map/ppermute | solution.py:29
  35.2 11.1 %collective-permute-start.56 = (f32[1,3,16]{2,1,0:T(4,128)S(1)}, f32[1,3,16]{2,1,0:T(4,128)S(1)}, u32[]{:S(2)}, u32[]{:S(2)}) collective-permute-start(f32[1,3,16]{2,1,0:T(4,128)S(1)} %pad_maximum_fusion.259), channel_id=1, source_target_pairs={{2,0},{3,1},{6,4},{7,5},{10,8},{11,9},{14,12},{15,13},{18,16},{19,... | collective-permute-start | bytes 584 | tf_op jit(solution)/shard_map/ppermute | solution.py:31
  36.5 11.1 %collective-permute-start.57 = (f32[1,3,16]{2,1,0:T(4,128)S(1)}, f32[1,3,16]{2,1,0:T(4,128)S(1)}, u32[]{:S(2)}, u32[]{:S(2)}) collective-permute-start(f32[1,3,16]{2,1,0:T(4,128)S(1)} %pad_maximum_fusion.259), channel_id=1, source_target_pairs={{0,2},{1,3},{4,6},{5,7},{8,10},{9,11},{12,14},{13,15},{16,18},{17,... | collective-permute-start | bytes 584 | tf_op jit(solution)/shard_map/ppermute | solution.py:29
  41.1 67.0 %all-to-all-start.1 = ((bf16[4,8,512]{2,1,0:T(8,128)(2,1)}), bf16[4,8,512]{2,1,0:T(8,128)(2,1)S(1)}, u32[]{:S(2)}, u32[]{:S(2)}) async-start(bf16[4,8,512]{2,1,0:T(8,128)(2,1)} %convert_element_type.15), calls=%async_computation.1 | async-start | bytes 65536 | tf_op jit(solution)/shard_map/all_to_all | solution.py:155
  46.3 7.3 %collective-permute-start.37 = (f32[2,1,32]{2,1,0:T(1,128)S(1)}, f32[2,1,32]{2,1,0:T(1,128)S(1)}, u32[]{:S(2)}, u32[]{:S(2)}) collective-permute-start(f32[2,1,32]{2,1,0:T(1,128)S(1)} %get-tuple-element.108), channel_id=1, source_target_pairs={{4,0},{8,4},{12,8},{5,1},{9,5},{13,9},{6,2},{10,6},{14,10},{7,3},{... | collective-permute-start | bytes 776 | tf_op jit(solution)/shard_map/ppermute | solution.py:31
  47.7 10.5 %collective-permute-start.42 = (f32[2,1,32]{2,1,0:T(1,128)S(1)}, f32[2,1,32]{2,1,0:T(1,128)S(1)}, u32[]{:S(2)}, u32[]{:S(2)}) collective-permute-start(f32[2,1,32]{2,1,0:T(1,128)S(1)} %broadcast.324), channel_id=1, source_target_pairs={{0,4},{4,8},{8,12},{1,5},{5,9},{9,13},{2,6},{6,10},{10,14},{3,7},{... | collective-permute-start | bytes 776 | tf_op jit(solution)/shard_map/ppermute | solution.py:29
  52.3 7.2 %collective-permute-start.43 = (f32[2,1,32]{2,1,0:T(1,128)S(1)}, f32[2,1,32]{2,1,0:T(1,128)S(1)}, u32[]{:S(2)}, u32[]{:S(2)}) collective-permute-start(f32[2,1,32]{2,1,0:T(1,128)S(1)} %broadcast.324), channel_id=1, source_target_pairs={{4,0},{8,4},{12,8},{5,1},{9,5},{13,9},{6,2},{10,6},{14,10},{7,3},{... | collective-permute-start | bytes 776 | tf_op jit(solution)/shard_map/ppermute | solution.py:31
  53.6 16.5 %collective-permute-start.18 = (f32[4,1,64]{2,1,0:T(1,128)S(1)}, f32[4,1,64]{2,1,0:T(1,128)S(1)}, u32[]{:S(2)}, u32[]{:S(2)}) collective-permute-start(f32[4,1,64]{2,1,0:T(1,128)S(1)} %get-tuple-element.70), channel_id=1, source_target_pairs={{0,4},{4,8},{8,12},{1,5},{5,9},{9,13},{2,6},{6,10},{10,14},{3,7},{... | collective-permute-start | bytes 3080 | tf_op jit(solution)/shard_map/ppermute | solution.py:29
  58.2 5.9 %collective-permute-start.38 = (f32[1,4,32]{2,1,0:T(4,128)S(1)}, f32[1,4,32]{2,1,0:T(4,128)S(1)}, u32[]{:S(2)}, u32[]{:S(2)}) collective-permute-start(f32[1,4,32]{2,1,0:T(4,128)S(1)} %get-tuple-element.98), channel_id=1, source_target_pairs={{2,0},{3,1},{6,4},{7,5},{10,8},{11,9},{14,12},{15,13},{18,16},{19,... | collective-permute-start | bytes 1544 | tf_op jit(solution)/shard_map/ppermute | solution.py:31
  59.5 5.9 %collective-permute-start.39 = (f32[1,4,32]{2,1,0:T(4,128)S(1)}, f32[1,4,32]{2,1,0:T(4,128)S(1)}, u32[]{:S(2)}, u32[]{:S(2)}) collective-permute-start(f32[1,4,32]{2,1,0:T(4,128)S(1)} %get-tuple-element.97), channel_id=1, source_target_pairs={{0,2},{1,3},{4,6},{5,7},{8,10},{9,11},{12,14},{13,15},{16,18},{17,... | collective-permute-start | bytes 1544 | tf_op jit(solution)/shard_map/ppermute | solution.py:29
  64.1 7.3 %collective-permute-start.19 = (f32[4,1,64]{2,1,0:T(1,128)S(1)}, f32[4,1,64]{2,1,0:T(1,128)S(1)}, u32[]{:S(2)}, u32[]{:S(2)}) collective-permute-start(f32[4,1,64]{2,1,0:T(1,128)S(1)} %get-tuple-element.71), channel_id=1, source_target_pairs={{4,0},{8,4},{12,8},{5,1},{9,5},{13,9},{6,2},{10,6},{14,10},{7,3},{... | collective-permute-start | bytes 3080 | tf_op jit(solution)/shard_map/ppermute | solution.py:31
  65.5 10.5 %collective-permute-start.24 = (f32[4,1,64]{2,1,0:T(1,128)S(1)}, f32[4,1,64]{2,1,0:T(1,128)S(1)}, u32[]{:S(2)}, u32[]{:S(2)}) collective-permute-start(f32[4,1,64]{2,1,0:T(1,128)S(1)} %broadcast.319), channel_id=1, source_target_pairs={{0,4},{4,8},{8,12},{1,5},{5,9},{9,13},{2,6},{6,10},{10,14},{3,7},{... | collective-permute-start | bytes 3080 | tf_op jit(solution)/shard_map/ppermute | solution.py:29
  70.1 7.2 %collective-permute-start.25 = (f32[4,1,64]{2,1,0:T(1,128)S(1)}, f32[4,1,64]{2,1,0:T(1,128)S(1)}, u32[]{:S(2)}, u32[]{:S(2)}) collective-permute-start(f32[4,1,64]{2,1,0:T(1,128)S(1)} %broadcast.319), channel_id=1, source_target_pairs={{4,0},{8,4},{12,8},{5,1},{9,5},{13,9},{6,2},{10,6},{14,10},{7,3},{... | collective-permute-start | bytes 3080 | tf_op jit(solution)/shard_map/ppermute | solution.py:31
  71.4 13.1 %collective-permute-start = (f32[8,1,128]{2,1,0:T(1,128)S(1)}, f32[8,1,128]{2,1,0:T(1,128)S(1)}, u32[]{:S(2)}, u32[]{:S(2)}) collective-permute-start(f32[8,1,128]{2,1,0:T(1,128)S(1)} %get-tuple-element.40), channel_id=1, source_target_pairs={{0,4},{4,8},{8,12},{1,5},{5,9},{9,13},{2,6},{6,10},{10,14},{3,7},{... | collective-permute-start | bytes 12296 | tf_op jit(solution)/shard_map/ppermute | solution.py:29
  76.0 5.9 %collective-permute-start.20 = (f32[1,6,64]{2,1,0:T(8,128)S(1)}, f32[1,6,64]{2,1,0:T(8,128)S(1)}, u32[]{:S(2)}, u32[]{:S(2)}) collective-permute-start(f32[1,6,64]{2,1,0:T(8,128)S(1)} %get-tuple-element.55), channel_id=1, source_target_pairs={{2,0},{3,1},{6,4},{7,5},{10,8},{11,9},{14,12},{15,13},{18,16},{19,... | collective-permute-start | bytes 4616 | tf_op jit(solution)/shard_map/ppermute | solution.py:31
  77.3 5.9 %collective-permute-start.21 = (f32[1,6,64]{2,1,0:T(8,128)S(1)}, f32[1,6,64]{2,1,0:T(8,128)S(1)}, u32[]{:S(2)}, u32[]{:S(2)}) collective-permute-start(f32[1,6,64]{2,1,0:T(8,128)S(1)} %get-tuple-element.54), channel_id=1, source_target_pairs={{0,2},{1,3},{4,6},{5,7},{8,10},{9,11},{12,14},{13,15},{16,18},{17,... | collective-permute-start | bytes 4616 | tf_op jit(solution)/shard_map/ppermute | solution.py:29
  83.2 216.5 %collective-permute-start.62 = (f32[1,3,16]{2,1,0:T(4,128)S(1)}, f32[1,3,16]{2,1,0:T(4,128)S(1)}, u32[]{:S(2)}, u32[]{:S(2)}) collective-permute-start(f32[1,3,16]{2,1,0:T(4,128)S(1)} %pad_maximum_fusion.260), channel_id=1, source_target_pairs={{2,0},{3,1},{6,4},{7,5},{10,8},{11,9},{14,12},{15,13},{18,16},{19,... | collective-permute-start | bytes 584 | tf_op jit(solution)/shard_map/ppermute | solution.py:31
  87.4 11.7 %collective-permute-start.2 = (f32[1,10,128]{2,1,0:T(8,128)S(1)}, f32[1,10,128]{2,1,0:T(8,128)S(1)}, u32[]{:S(2)}, u32[]{:S(2)}) collective-permute-start(f32[1,10,128]{2,1,0:T(8,128)S(1)} %get-tuple-element.33), channel_id=1, source_target_pairs={{2,0},{3,1},{6,4},{7,5},{10,8},{11,9},{14,12},{15,13},{18,16},{19,... | collective-permute-start | bytes 15368 | tf_op jit(solution)/shard_map/ppermute | solution.py:31
  88.7 10.5 %collective-permute-start.3 = (f32[1,10,128]{2,1,0:T(8,128)S(1)}, f32[1,10,128]{2,1,0:T(8,128)S(1)}, u32[]{:S(2)}, u32[]{:S(2)}) collective-permute-start(f32[1,10,128]{2,1,0:T(8,128)S(1)} %get-tuple-element.32), channel_id=1, source_target_pairs={{0,2},{1,3},{4,6},{5,7},{8,10},{9,11},{12,14},{13,15},{16,18},{17,... | collective-permute-start | bytes 15368 | tf_op jit(solution)/shard_map/ppermute | solution.py:29
  93.3 10.3 %collective-permute-start.8 = (f32[1,10,128]{2,1,0:T(8,128)S(1)}, f32[1,10,128]{2,1,0:T(8,128)S(1)}, u32[]{:S(2)}, u32[]{:S(2)}) collective-permute-start(f32[1,10,128]{2,1,0:T(8,128)S(1)} %get-tuple-element.35), channel_id=1, source_target_pairs={{2,0},{3,1},{6,4},{7,5},{10,8},{11,9},{14,12},{15,13},{18,16},{19,... | collective-permute-start | bytes 15368 | tf_op jit(solution)/shard_map/ppermute | solution.py:31
  94.6 9.0 %collective-permute-start.9 = (f32[1,10,128]{2,1,0:T(8,128)S(1)}, f32[1,10,128]{2,1,0:T(8,128)S(1)}, u32[]{:S(2)}, u32[]{:S(2)}) collective-permute-start(f32[1,10,128]{2,1,0:T(8,128)S(1)} %get-tuple-element.34), channel_id=1, source_target_pairs={{0,2},{1,3},{4,6},{5,7},{8,10},{9,11},{12,14},{13,15},{16,18},{17,... | collective-permute-start | bytes 15368 | tf_op jit(solution)/shard_map/ppermute | solution.py:29
  99.3 122.3 %collective-permute-start.4 = (f32[10,10,1]{2,1,0:T(8,128)S(1)}, f32[10,10,1]{2,1,0:T(8,128)S(1)}, u32[]{:S(2)}, u32[]{:S(2)}) collective-permute-start(f32[10,10,1]{2,1,0:T(8,128)S(1)} %get-tuple-element.25), channel_id=1, source_target_pairs={{1,0},{3,2},{5,4},{7,6},{9,8},{11,10},{13,12},{15,14},{17,16},{19,... | collective-permute-start | bytes 1208 | tf_op jit(solution)/shard_map/ppermute | solution.py:31
  100.6 122.3 %collective-permute-start.5 = (f32[10,10,1]{2,1,0:T(8,128)S(1)}, f32[10,10,1]{2,1,0:T(8,128)S(1)}, u32[]{:S(2)}, u32[]{:S(2)}) collective-permute-start(f32[10,10,1]{2,1,0:T(8,128)S(1)} %get-tuple-element.24), channel_id=1, source_target_pairs={{0,1},{2,3},{4,5},{6,7},{8,9},{10,11},{12,13},{14,15},{16,17},{18,... | collective-permute-start | bytes 1208 | tf_op jit(solution)/shard_map/ppermute | solution.py:29
  103.8 120.5 %collective-permute-start.10 = (f32[10,10,1]{2,1,0:T(8,128)S(1)}, f32[10,10,1]{2,1,0:T(8,128)S(1)}, u32[]{:S(2)}, u32[]{:S(2)}) collective-permute-start(f32[10,10,1]{2,1,0:T(8,128)S(1)} %get-tuple-element.26), channel_id=1, source_target_pairs={{1,0},{3,2},{5,4},{7,6},{9,8},{11,10},{13,12},{15,14},{17,16},{19,... | collective-permute-start | bytes 1208 | tf_op jit(solution)/shard_map/ppermute | solution.py:31
  105.1 119.2 %collective-permute-start.11 = (f32[10,10,1]{2,1,0:T(8,128)S(1)}, f32[10,10,1]{2,1,0:T(8,128)S(1)}, u32[]{:S(2)}, u32[]{:S(2)}) collective-permute-start(f32[10,10,1]{2,1,0:T(8,128)S(1)} %get-tuple-element.27), channel_id=1, source_target_pairs={{0,1},{2,3},{4,5},{6,7},{8,9},{10,11},{12,13},{14,15},{16,17},{18,... | collective-permute-start | bytes 1208 | tf_op jit(solution)/shard_map/ppermute | solution.py:29
  221.6 79.4 %collective-permute-start.63 = (f32[1,3,16]{2,1,0:T(4,128)S(1)}, f32[1,3,16]{2,1,0:T(4,128)S(1)}, u32[]{:S(2)}, u32[]{:S(2)}) collective-permute-start(f32[1,3,16]{2,1,0:T(4,128)S(1)} %pad_maximum_fusion.260), channel_id=1, source_target_pairs={{0,2},{1,3},{4,6},{5,7},{8,10},{9,11},{12,14},{13,15},{16,18},{17,... | collective-permute-start | bytes 584 | tf_op jit(solution)/shard_map/ppermute | solution.py:29
  222.9 44.0 %collective-permute-start.44 = (f32[1,4,32]{2,1,0:T(4,128)S(1)}, f32[1,4,32]{2,1,0:T(4,128)S(1)}, u32[]{:S(2)}, u32[]{:S(2)}) collective-permute-start(f32[1,4,32]{2,1,0:T(4,128)S(1)} %get-tuple-element.100), channel_id=1, source_target_pairs={{2,0},{3,1},{6,4},{7,5},{10,8},{11,9},{14,12},{15,13},{18,16},{19,... | collective-permute-start | bytes 1544 | tf_op jit(solution)/shard_map/ppermute | solution.py:31
  229.7 8.7 %collective-permute-start.26 = (f32[1,6,64]{2,1,0:T(8,128)S(1)}, f32[1,6,64]{2,1,0:T(8,128)S(1)}, u32[]{:S(2)}, u32[]{:S(2)}) collective-permute-start(f32[1,6,64]{2,1,0:T(8,128)S(1)} %get-tuple-element.57), channel_id=1, source_target_pairs={{2,0},{3,1},{6,4},{7,5},{10,8},{11,9},{14,12},{15,13},{18,16},{19,... | collective-permute-start | bytes 4616 | tf_op jit(solution)/shard_map/ppermute | solution.py:31
  238.4 5.9 %collective-permute-start.14 = (f32[1,10,128]{2,1,0:T(8,128)S(1)}, f32[1,10,128]{2,1,0:T(8,128)S(1)}, u32[]{:S(2)}, u32[]{:S(2)}) collective-permute-start(f32[1,10,128]{2,1,0:T(8,128)S(1)} %get-tuple-element.31), channel_id=1, source_target_pairs={{2,0},{3,1},{6,4},{7,5},{10,8},{11,9},{14,12},{15,13},{18,16},{19,... | collective-permute-start | bytes 15368 | tf_op jit(solution)/shard_map/ppermute | solution.py:31
  239.7 5.9 %collective-permute-start.15 = (f32[1,10,128]{2,1,0:T(8,128)S(1)}, f32[1,10,128]{2,1,0:T(8,128)S(1)}, u32[]{:S(2)}, u32[]{:S(2)}) collective-permute-start(f32[1,10,128]{2,1,0:T(8,128)S(1)} %get-tuple-element.30), channel_id=1, source_target_pairs={{0,2},{1,3},{4,6},{5,7},{8,10},{9,11},{12,14},{13,15},{16,18},{17,... | collective-permute-start | bytes 15368 | tf_op jit(solution)/shard_map/ppermute | solution.py:29
  250.1 6.8 %collective-permute-start.22 = (f32[6,6,1]{2,1,0:T(8,128)S(1)}, f32[6,6,1]{2,1,0:T(8,128)S(1)}, u32[]{:S(2)}, u32[]{:S(2)}) collective-permute-start(f32[6,6,1]{2,1,0:T(8,128)S(1)} %get-tuple-element.47), channel_id=1, source_target_pairs={{1,0},{3,2},{5,4},{7,6},{9,8},{11,10},{13,12},{15,14},{17,16},{19,... | collective-permute-start | bytes 440 | tf_op jit(solution)/shard_map/ppermute | solution.py:31
  251.4 6.8 %collective-permute-start.23 = (f32[6,6,1]{2,1,0:T(8,128)S(1)}, f32[6,6,1]{2,1,0:T(8,128)S(1)}, u32[]{:S(2)}, u32[]{:S(2)}) collective-permute-start(f32[6,6,1]{2,1,0:T(8,128)S(1)} %get-tuple-element.46), channel_id=1, source_target_pairs={{0,1},{2,3},{4,5},{6,7},{8,9},{10,11},{12,13},{14,15},{16,17},{18,... | collective-permute-start | bytes 440 | tf_op jit(solution)/shard_map/ppermute | solution.py:29
  258.3 7.2 %collective-permute-start.29 = (f32[6,6,1]{2,1,0:T(8,128)S(1)}, f32[6,6,1]{2,1,0:T(8,128)S(1)}, u32[]{:S(2)}, u32[]{:S(2)}) collective-permute-start(f32[6,6,1]{2,1,0:T(8,128)S(1)} %get-tuple-element.49), channel_id=1, source_target_pairs={{0,1},{2,3},{4,5},{6,7},{8,9},{10,11},{12,13},{14,15},{16,17},{18,... | collective-permute-start | bytes 440 | tf_op jit(solution)/shard_map/ppermute | solution.py:29
  261.3 8.5 %collective-permute-start.45 = (f32[1,4,32]{2,1,0:T(4,128)S(1)}, f32[1,4,32]{2,1,0:T(4,128)S(1)}, u32[]{:S(2)}, u32[]{:S(2)}) collective-permute-start(f32[1,4,32]{2,1,0:T(4,128)S(1)} %get-tuple-element.99), channel_id=1, source_target_pairs={{0,2},{1,3},{4,6},{5,7},{8,10},{9,11},{12,14},{13,15},{16,18},{17,... | collective-permute-start | bytes 1544 | tf_op jit(solution)/shard_map/ppermute | solution.py:29
  265.5 53.0 %collective-permute-start.58 = (f32[3,3,1]{2,1,0:T(4,128)S(1)}, f32[3,3,1]{2,1,0:T(4,128)S(1)}, u32[]{:S(2)}, u32[]{:S(2)}) collective-permute-start(f32[3,3,1]{2,1,0:T(4,128)S(1)} %get-tuple-element.87), channel_id=1, source_target_pairs={{1,0},{3,2},{5,4},{7,6},{9,8},{11,10},{13,12},{15,14},{17,16},{19,... | collective-permute-start | bytes 116 | tf_op jit(solution)/shard_map/ppermute | solution.py:31
  275.3 5.9 %collective-permute-start.32 = (f32[1,6,64]{2,1,0:T(8,128)S(1)}, f32[1,6,64]{2,1,0:T(8,128)S(1)}, u32[]{:S(2)}, u32[]{:S(2)}) collective-permute-start(f32[1,6,64]{2,1,0:T(8,128)S(1)} %get-tuple-element.53), channel_id=1, source_target_pairs={{2,0},{3,1},{6,4},{7,5},{10,8},{11,9},{14,12},{15,13},{18,16},{19,... | collective-permute-start | bytes 4616 | tf_op jit(solution)/shard_map/ppermute | solution.py:31
  296.1 22.5 %collective-permute-start.59 = (f32[3,3,1]{2,1,0:T(4,128)S(1)}, f32[3,3,1]{2,1,0:T(4,128)S(1)}, u32[]{:S(2)}, u32[]{:S(2)}) collective-permute-start(f32[3,3,1]{2,1,0:T(4,128)S(1)} %get-tuple-element.86), channel_id=1, source_target_pairs={{0,1},{2,3},{4,5},{6,7},{8,9},{10,11},{12,13},{14,15},{16,17},{18,... | collective-permute-start | bytes 116 | tf_op jit(solution)/shard_map/ppermute | solution.py:29
  305.2 7.2 %collective-permute-start.50 = (f32[1,4,32]{2,1,0:T(4,128)S(1)}, f32[1,4,32]{2,1,0:T(4,128)S(1)}, u32[]{:S(2)}, u32[]{:S(2)}) collective-permute-start(f32[1,4,32]{2,1,0:T(4,128)S(1)} %get-tuple-element.96), channel_id=1, source_target_pairs={{2,0},{3,1},{6,4},{7,5},{10,8},{11,9},{14,12},{15,13},{18,16},{19,... | collective-permute-start | bytes 1544 | tf_op jit(solution)/shard_map/ppermute | solution.py:31
  306.5 5.9 %collective-permute-start.51 = (f32[1,4,32]{2,1,0:T(4,128)S(1)}, f32[1,4,32]{2,1,0:T(4,128)S(1)}, u32[]{:S(2)}, u32[]{:S(2)}) collective-permute-start(f32[1,4,32]{2,1,0:T(4,128)S(1)} %get-tuple-element.95), channel_id=1, source_target_pairs={{0,2},{1,3},{4,6},{5,7},{8,10},{9,11},{12,14},{13,15},{16,18},{17,... | collective-permute-start | bytes 1544 | tf_op jit(solution)/shard_map/ppermute | solution.py:29
  311.2 7.4 %collective-permute-start.64 = (f32[3,3,1]{2,1,0:T(4,128)S(1)}, f32[3,3,1]{2,1,0:T(4,128)S(1)}, u32[]{:S(2)}, u32[]{:S(2)}) collective-permute-start(f32[3,3,1]{2,1,0:T(4,128)S(1)} %get-tuple-element.88), channel_id=1, source_target_pairs={{1,0},{3,2},{5,4},{7,6},{9,8},{11,10},{13,12},{15,14},{17,16},{19,... | collective-permute-start | bytes 116 | tf_op jit(solution)/shard_map/ppermute | solution.py:31
  507.7 5.9 %collective-permute-start.123 = (f32[1,10,128]{2,1,0:T(8,128)S(1)}, f32[1,10,128]{2,1,0:T(8,128)S(1)}, u32[]{:S(2)}, u32[]{:S(2)}) collective-permute-start(f32[1,10,128]{2,1,0:T(8,128)S(1)} %get-tuple-element.28), channel_id=1, source_target_pairs={{0,2},{1,3},{4,6},{5,7},{8,10},{9,11},{12,14},{13,15},{16,18},{17,... | collective-permute-start | bytes 15368 | tf_op jit(solution)/shard_map/ppermute | solution.py:29
  (87 other events, 614.8 us)
where the time goes:
time: 523 us; the launch traced here: 520 us
  starting transfers between devices  307 us (59%)
  other arithmetic  120 us (23%)
  waiting for transfers between devices  79.6 us (15%)
  local copies, waits for them, and re-layouts  11 us (2%)
    ppermute x63, starting transfers between devices, padded_2(): lax.ppermute(tail, axis, [(i, (i + 1) % count) for i in range(ends)])  216 us
    scatter-add x1, other arithmetic, per_device(): density = charge_density.reshape(-1).at[targets.reshape(-1)].add(deposits...  113 us
    ppermute x63, starting transfers between devices, padded_2(): lax.ppermute(head, axis, [((i + 1) % count, i) for i in range(ends)])  81.2 us
    ppermute x63, waiting for transfers between devices, padded_2(): lax.ppermute(head, axis, [((i + 1) % count, i) for i in range(ends)])  55.5 us
    ppermute x63, waiting for transfers between devices, padded_2(): lax.ppermute(tail, axis, [(i, (i + 1) % count) for i in range(ends)])  24.1 us
  transfers between devices with their start and end apart: 128, of which 37 were waited for; matrix products, arithmetic and copies ran while one was open for 24% of the time, Pallas kernels for 0%

commit v1 on v0

v1 whole, which is shorter than its diff:
```python
import functools
import math

import jax
import jax.numpy as jnp
from jax import lax
from jax.experimental import pallas as pl
from jax.experimental.pallas import tpu as pltpu
from jax.sharding import PartitionSpec as P

PATCH = 8
CAP = 8
NU_COARSE = 8
MESH = pl.DeviceIdType.MESH

four_pi = 4.0 * math.pi
relax_weight = 2.0 / 3.0
gauss_norm = (2.0 * math.pi) ** 1.5


def iota(shape, dim):
    return lax.broadcasted_iota(jnp.int32, shape, dim)


def each(count, body):
    if count <= 16:
        for k in range(1, count):
            body(k)
    else:
        lax.fori_loop(1, count, lambda k, c: (body(k), c)[1], 0)


def rolled(values, step, dim):
    return pltpu.roll(values, step % values.shape[dim], dim)


def pair_sum_z(values, step):
    low = (iota(values.shape, 2) // step) % 2 == 0
    return values + jnp.where(low, rolled(values, -step, 2), rolled(values, step, 2))


def pair_sum_x(values):
    a, b, c = values.shape
    v = values.reshape(a // 2, 2, b, c)
    return v[:, 0] + v[:, 1]


def repeat_x(values):
    a, b, c = values.shape
    return jnp.broadcast_to(values[:, None], (a, 2, b, c)).reshape(2 * a, b, c)


def shifted_x(values, step):
    zero = jnp.zeros_like(values[:1])
    if step > 0:
        return jnp.concatenate([values[1:], zero], 0)
    return jnp.concatenate([zero, values[:-1]], 0)


class Coarse:
    def __init__(self, eps, level, sy, sz):
        self.sy, self.sz = sy, sz
        self.spacing = 1.0 / 4.0**level
        y, z = iota(eps.shape, 1), iota(eps.shape, 2)
        ny, nz = eps.shape[1], eps.shape[2]
        xp, xm = shifted_x(eps, 1), shifted_x(eps, -1)
        in_y, in_z = y < ny - sy, z < nz - sz
        yp = jnp.where(in_y, rolled(eps, -sy, 1), 0.0)
        ym = jnp.where(y >= sy, rolled(eps, sy, 1), 0.0)
        zp = jnp.where(in_z, rolled(eps, -sz, 2), 0.0)
        zm = jnp.where(z >= sz, rolled(eps, sz, 2), 0.0)
        weight_sum = 0.5 * (6.0 * eps + xp + xm + yp + ym + zp + zm)
        self.inverse = (relax_weight / self.spacing) / weight_sum
        self.wx = 0.5 * (eps + xp)
        self.wy = jnp.where(in_y, 0.5 * (eps + yp), 0.0)
        self.wz = jnp.where(in_z, 0.5 * (eps + zp), 0.0)

    def beside(self, f):
        out = self.wx * shifted_x(f, 1) + shifted_x(self.wx * f, -1)
        out += self.wy * rolled(f, -self.sy, 1) + rolled(self.wy * f, self.sy, 1)
        out += self.wz * rolled(f, -self.sz, 2) + rolled(self.wz * f, self.sz, 2)
        return self.spacing * out

    def first(self, g):
        return self.inverse * g

    def residual_of_first(self, g, f):
        return (1.0 / 3.0) * g + self.beside(f)

    def sweep(self, g, f):
        return (1.0 / 3.0) * f + self.inverse * (g + self.beside(f))


def around(values, halo):
    (xl, xh), (yl, yh), (zl, zh) = halo
    y, z = iota(values.shape, 1), iota(values.shape, 2)
    ny, nz = values.shape[1], values.shape[2]
    shape = values.shape
    return (
        jnp.concatenate([values[1:], xh[None]], 0),
        jnp.concatenate([xl[None], values[:-1]], 0),
        jnp.where(y == ny - 1, jnp.broadcast_to(yh, shape), rolled(values, -1, 1)),
        jnp.where(y == 0, jnp.broadcast_to(yl, shape), rolled(values, 1, 1)),
        jnp.where(z == nz - 1, rolled(zh, -1, 2), rolled(values, -1, 2)),
        jnp.where(z == 0, rolled(zl, 1, 2), rolled(values, 1, 2)),
    )


def kernel(
    sizes,
    charge_ref, eps_ref, centers_ref, widths_ref, charges_ref, counts_ref, anchors_ref,
    out_ref,
    f_ref, hx_ref, hy_ref, hz_ref, sy_ref, pairs_ref, gather_ref, ions_out, ions_in, whole1, half2, up1, up0,
    face_send, face_recv, gather_send, gather_recv, ion_send, ion_recv,
):
    ngx, ngy, ngz = sizes
    cx, cy, cz = charge_ref.shape
    bx, by = cx // 2, cy // 2
    n = ngx * ngy * ngz
    gx, gy, gz = lax.axis_index("gx"), lax.axis_index("gy"), lax.axis_index("gz")
    me = (gx * ngy + gy) * ngz + gz

    def peer(k):
        at = (me + k) % n
        return {"gx": at // (ngy * ngz), "gy": (at // ngz) % ngy, "gz": at % ngz}

    barrier = pltpu.get_barrier_semaphore()
    each(n, lambda k: pl.semaphore_signal(barrier, inc=1, device_id=peer(k), device_id_type=MESH))

    axes = (("gx", gx, ngx), ("gy", gy, ngy), ("gz", gz, ngz))
    halos = (hx_ref, hy_ref, hz_ref)
    for axis in range(3):
        name, at, count = axes[axis]
        for side, missing in ((0, at == 0), (1, at == count - 1)):
            @pl.when(missing)
            def _(axis=axis, side=side):
                for kind in range(2):
                    buffer = halos[axis].at[kind, side]
                    buffer[...] = jnp.zeros(buffer.shape, jnp.float32)

    def face_copy(kind, axis, side, source):
        name, at, count = axes[axis]
        target = at + 1 if side == 0 else at - 1
        index = (kind * 3 + axis) * 2 + side
        return pltpu.make_async_remote_copy(
            src_ref=source, dst_ref=halos[axis].at[kind, side],
            send_sem=face_send.at[index], recv_sem=face_recv.at[index],
            device_id={name: target}, device_id_type=MESH)

    def face_sources(kind, field):
        return (
            (field.at[cx - 1], field.at[0]),
            (sy_ref.at[kind, 0], sy_ref.at[kind, 1]),
            (field, field),
        )

    def send_faces(kind, field):
        sy_ref[kind, 0] = field[:, cy - 1 : cy, :]
        sy_ref[kind, 1] = field[:, 0:1, :]
        sources = face_sources(kind, field)
        for axis in range(3):
            at, count = axes[axis][1:]
            for side in range(2):
                @pl.when((at < count - 1) if side == 0 else (at > 0))
                def _(axis=axis, side=side):
                    face_copy(kind, axis, side, sources[axis][side]).start()

    def wait_faces(kind, field, sent):
        sources = face_sources(kind, field)
        for axis in range(3):
            at, count = axes[axis][1:]
            for side in range(2):
                up = (side == 0) == sent
                @pl.when((at < count - 1) if up else (at > 0))
                def _(axis=axis, side=side):
                    copy = face_copy(kind, axis, side, sources[axis][side])
                    copy.wait_send() if sent else copy.wait_recv()

    def gather_copy(kind, k):
        return pltpu.make_async_remote_copy(
            src_ref=gather_ref.at[kind, me], dst_ref=gather_ref.at[kind, me],
            send_sem=gather_send.at[kind, k], recv_sem=gather_recv.at[kind, k],
            device_id=peer(k), device_id_type=MESH)

    def ion_copy(k):
        to = (gy + k) % ngy
        return pltpu.make_async_remote_copy(
            src_ref=ions_out.at[to], dst_ref=ions_in.at[gy],
            send_sem=ion_send.at[k], recv_sem=ion_recv.at[k],
            device_id={"gy": to}, device_id_type=MESH)

    def restrict(values):
        pairs_ref[...] = pair_sum_z(pair_sum_x(values), 1)
        return 0.125 * (pairs_ref[:, pl.ds(0, by, stride=2), :] + pairs_ref[:, pl.ds(1, by, stride=2), :])

    def assemble(kind):
        for a in range(ngx):
            for b in range(ngy):
                for c in range(ngz):
                    whole1[a * bx : (a + 1) * bx, b * by : (b + 1) * by, c * cz : (c + 1) * cz] = gather_ref[
                        kind, (a * ngy + b) * ngz + c]
        return whole1[...]

    eps = eps_ref[...]
    gather_ref[0, me] = restrict(eps)
    counts = counts_ref[...]
    for d in range(ngy):
        for c in range(3):
            ions_out[d, c : c + 1, 0:CAP] = centers_ref[c, d : d + 1, :]
        ions_out[d, 3:4, 0:CAP] = widths_ref[d : d + 1, :]
        live = iota((1, CAP), 1) < jnp.broadcast_to(counts[:, d : d + 1], (1, CAP))
        ions_out[d, 4:5, 0:CAP] = jnp.where(live, charges_ref[d : d + 1, :], 0.0)
        ions_out[d, 5:6, 0:CAP] = anchors_ref[2, d : d + 1, :].astype(jnp.float32)
        ions_out[d, 6:8, 0:CAP] = jnp.zeros((2, CAP), jnp.float32)
        ions_out[d, :, CAP:] = jnp.ones((8, 128 - CAP), jnp.float32)
    ions_in[gy] = ions_out[gy]
    up0[...] = jnp.zeros_like(up0)

    pl.semaphore_wait(barrier, n - 1)
    each(ngy, lambda k: ion_copy(k).start())
    send_faces(0, eps_ref)
    each(n, lambda k: gather_copy(0, k).start())

    each(ngy, lambda k: ion_copy(k).wait_recv())

    def deposit(source, density):
        tile = ions_in[source]
        lines = tile.T[0:CAP]
        u, v, s, q = tile[0:1], tile[1:2], tile[3:4], tile[4:5]
        decay = 0.5 / (s * s)
        amplitude = q / (gauss_norm * s * s * s)
        j = iota((cy, 128), 0).astype(jnp.float32)
        along_y = jnp.exp(-((j - v) ** 2) * decay)
        flat = jnp.stack(
            [(amplitude * jnp.exp(-((float(i) - u) ** 2) * decay)) * along_y for i in range(cx)])
        w, spread, anchor = lines[:, 2:3], lines[:, 3:4], lines[:, 5:6]
        position = iota((CAP, cz), 1).astype(jnp.float32) - anchor
        along_z = jnp.exp(-((position - w) ** 2) * (0.5 / (spread * spread)))
        along_z = jnp.where((position >= 0.0) & (position < float(PATCH)), along_z, 0.0)
        for e in range(CAP):
            block = flat[:, :, e : e + 1] * along_z[None, e : e + 1, :]
            density += block.astype(jnp.bfloat16).astype(jnp.float32)
        return density

    density = charge_ref[...]
    if ngy <= 4:
        for source in range(ngy):
            density = deposit(source, density)
    else:
        density = lax.fori_loop(0, ngy, deposit, density)
    g = four_pi * density

    wait_faces(0, eps_ref, False)

    def halo(kind):
        return tuple((buffer[kind, 0], buffer[kind, 1]) for buffer in halos)

    eps_around = around(eps, halo(0))
    weight_sum = 0.5 * (6.0 * eps + sum(eps_around[1:], eps_around[0]))
    weights = [0.5 * (eps + other) for other in eps_around]
    inverse = relax_weight / weight_sum
    f = inverse * g
    f_ref[...] = f
    send_faces(1, f_ref)

    each(n, lambda k: gather_copy(0, k).wait_recv())
    nx1, ny1 = whole1.shape[:2]

    def down_y(values):
        rows = ny1 // 2
        parts = []
        for c in range(ngz):
            half2[c] = values[:, :, c * cz : (c + 1) * cz]
            parts.append(half2[c, :, pl.ds(0, rows, stride=2), :] + half2[c, :, pl.ds(1, rows, stride=2), :])
        return jnp.concatenate(parts, 2)

    def pair_sum_y(values):
        low = iota(values.shape, 1) % 2 == 0
        return values + jnp.where(low, rolled(values, -1, 1), rolled(values, 1, 1))

    def restrict_1(values):
        return 0.125 * down_y(pair_sum_z(pair_sum_x(values), 2))

    def restrict_2(values):
        return 0.125 * pair_sum_y(pair_sum_z(pair_sum_x(values), 4))

    eps1 = assemble(0)
    eps2 = restrict_1(eps1)
    eps3 = restrict_2(eps2)
    level1, level2, level3 = Coarse(eps1, 1, 1, 2), Coarse(eps2, 2, 1, 4), Coarse(eps3, 3, 2, 8)

    wait_faces(1, f_ref, False)

    def beside(values, halo_values):
        total = None
        for weight, other in zip(weights, around(values, halo_values)):
            total = weight * other if total is None else total + weight * other
        return total

    f_halo = halo(1)
    gather_ref[1, me] = restrict((1.0 / 3.0) * g + beside(f, f_halo))
    each(n, lambda k: gather_copy(1, k).start())
    each(n, lambda k: gather_copy(1, k).wait_recv())

    g1 = assemble(1)
    f1 = level1.first(g1)
    g2 = restrict_1(level1.residual_of_first(g1, f1))
    f2 = level2.first(g2)
    g3 = restrict_2(level2.residual_of_first(g2, f2))
    f3 = level3.first(g3)
    for _ in range(NU_COARSE - 1):
        f3 = level3.sweep(g3, f3)
    f2 = level2.sweep(g2, f2 + repeat_x(f3))
    fine2 = repeat_x(f2)
    for c in range(ngz):
        for odd in range(2):
            up1[c, :, pl.ds(odd, ny1 // 2, stride=2), :] = fine2[:, :, c * cz : (c + 1) * cz]
    f1 = level1.sweep(g1, f1 + jnp.concatenate([up1[c] for c in range(ngz)], 2))
    for c in range(ngz):
        for odd in range(2):
            up0[c + 1, 1 : nx1 + 1, pl.ds(cy + odd, ny1, stride=2), :] = f1[:, :, c * cz : (c + 1) * cz]

    def part(dx, lx, dy, dz):
        return up0[gz + dz, pl.ds(gx * bx + dx, lx), pl.ds(pl.multiple_of((gy + dy) * cy, cy), cy), :]

    (xl, xh), (yl, yh), (zl, zh) = f_halo
    f = f + repeat_x(part(1, bx, 1, 1))
    f_halo = (
        (xl + part(0, 1, 1, 1)[0], xh + part(bx + 1, 1, 1, 1)[0]),
        (yl + repeat_x(part(1, bx, 0, 1)[:, cy - 1 : cy, :]), yh + repeat_x(part(1, bx, 2, 1)[:, 0:1, :])),
        (zl + repeat_x(part(1, bx, 1, 0)), zh + repeat_x(part(1, bx, 1, 2))),
    )
    out_ref[...] = (1.0 / 3.0) * f + inverse * (g + beside(f, f_halo))

    each(ngy, lambda k: ion_copy(k).wait_send())
    wait_faces(0, eps_ref, True)
    wait_faces(1, f_ref, True)
    each(n, lambda k: gather_copy(0, k).wait_send())
    each(n, lambda k: gather_copy(1, k).wait_send())


def solution(mesh):
    ngx, ngy, ngz = mesh.shape["gx"], mesh.shape["gy"], mesh.shape["gz"]

    def per_device(charge_density, permittivity, ion_centers, ion_widths, ion_charges, block_counts, block_anchors):
        cx, cy, cz = charge_density.shape
        n = ngx * ngy * ngz
        nx1, ny1 = ngx * cx // 2, ngy * cy // 2
        f32 = jnp.float32
        dma = pltpu.SemaphoreType.DMA
        return pl.pallas_call(
            functools.partial(kernel, (ngx, ngy, ngz)),
            out_shape=jax.ShapeDtypeStruct((cx, cy, cz), f32),
            in_specs=[pl.BlockSpec(memory_space=pltpu.VMEM)] * 7,
            out_specs=pl.BlockSpec(memory_space=pltpu.VMEM),
            scratch_shapes=[
                pltpu.VMEM((cx, cy, cz), f32),
                pltpu.VMEM((2, 2, cy, cz), f32),
                pltpu.VMEM((2, 2, cx, 1, cz), f32),
                pltpu.VMEM((2, 2, cx, cy, cz), f32),
                pltpu.VMEM((2, 2, cx, 1, cz), f32),
                pltpu.VMEM((cx // 2, cy, cz), f32),
                pltpu.VMEM((2, n, cx // 2, cy // 2, cz), f32),
                pltpu.VMEM((ngy, 8, 128), f32),
                pltpu.VMEM((ngy, 8, 128), f32),
                pltpu.VMEM((nx1, ny1, ngz * cz), f32),
                pltpu.VMEM((ngz, nx1 // 2, ny1, cz), f32),
                pltpu.VMEM((ngz, nx1, ny1, cz), f32),
                pltpu.VMEM((ngz + 2, nx1 + 2, (ngy + 2) * cy, cz), f32),
                dma((12,)), dma((12,)), dma((2, n)), dma((2, n)), dma((ngy,)), dma((ngy,)),
            ],
            compiler_params=pltpu.CompilerParams(
                collective_id=0, has_side_effects=True, vmem_limit_bytes=48 * 1024 * 1024),
        )(
            charge_density,
            permittivity,
            ion_centers.reshape(3, ngy, CAP),
            ion_widths.reshape(ngy, CAP),
            ion_charges.reshape(ngy, CAP),
            block_counts.reshape(1, ngy),
            block_anchors.reshape(3, ngy, CAP),
        )

    field = P(("groups", "gx"), "gy", "gz")
    return jax.shard_map(
        per_device, mesh=mesh, in_specs=(field,) * 7, out_specs=field, check_vma=False)
```

time: 523 us -> 24.1 us (0.05)
  starting transfers between devices: 307 us -> 0 us
  other arithmetic: 120 us -> 0 us
  waiting for transfers between devices: 79.6 us -> 0 us
  Pallas kernels: 0 us -> 19.5 us
  local copies, waits for them, and re-layouts: 11 us -> 4.2 us
    ppermute x126 -> x0, starting transfers between devices: 298 us -> none  [the longest x63 216 us: padded_2(): lax.ppermute(tail, axis, [(i, (i + 1) % count) for i in range(ends)])]
    scatter-add x1 -> x0, other arithmetic: 113 us -> none  [per_device(): density = charge_density.reshape(-1).at[targets.reshape(-1)].add(deposits...]
    ppermute x126 -> x0, waiting for transfers between devices: 79.6 us -> none  [the longest x63 55.5 us: padded_2(): lax.ppermute(head, axis, [((i + 1) % count, i) for i in range(ends)])]
    pallas_call x0 -> x1, Pallas kernels: none -> 19.5 us  [per_device(): pl.pallas_call(functools.partial(kernel, (ngx, ngy, ngz)), out_shape=jax....]
    all_to_all x2 -> x0, starting transfers between devices: 9.58 us -> none  [the longest x1 5.94 us: per_device(): lax.all_to_all(anchor_flat, 'gy', split_axis=0, concat_axis=0, tiled=True)]
    reshape x8 -> x0, local copies, waits for them, and re-layouts: 5.81 us -> none  [the longest x3 5.19 us: restrict_mean(): values.reshape(size_a // 2, 2, size_b // 2, 2, size_c // 2, 2)]
  transfers between devices with their start and end apart: 128 -> 0, of which waited for: 37 -> 0; matrix products, arithmetic and copies ran while one was open for 24% -> 0% of each run, Pallas kernels for 0% -> 0%
where the time goes in v1:
time: 24.1 us; the launch traced here: 23.7 us
  Pallas kernels  19.5 us (81%)
  local copies, waits for them, and re-layouts  4.2 us (17%)
    pallas_call x1, Pallas kernels, per_device(): pl.pallas_call(functools.partial(kernel, (ngx, ngy, ngz)), out_shape=jax....  19.5 us
    unnamed x15, local copies, waits for them, and re-layouts  4.2 us

profile of v1, /device:TPU:0, one launch (start us, length us, event | category | flops | bytes accessed | tf_op | source)
XLA Modules:
  0.0 23.7 jit_solution(10342674160463994658)
XLA Ops:
  0.0 0.0 copy-start.2
  0.0 0.0 copy-start.4
  0.0 0.0 copy-start.6
  0.0 0.7 %copy-done.2 = f32[1,1,1,3,4,8]{5,4,3,2,1,0:T(4,128)S(1)} copy-done((f32[1,1,1,3,4,8]{5,4,3,2,1,0:T(4,128)S(1)}, f32[1,1,1,3,4,8]{5,4,3,2,1,0:T(4,128)}, u32[]{:S(2)}) %copy-start.2) | copy-done | bytes 408
  0.7 0.0 copy-done.4
  0.7 0.0 copy-done.6
  0.7 0.0 copy-start
  0.7 0.8 %copy-done = f32[8,8,128]{2,1,0:T(8,128)S(1)} copy-done((f32[8,8,128]{2,1,0:T(8,128)S(1)}, f32[8,8,128]{2,1,0:T(8,128)}, u32[]{:S(2)}) %copy-start) | copy-done | bytes 32792
  1.5 0.0 copy-start.1
  1.5 0.8 %copy-done.1 = f32[8,8,128]{2,1,0:T(8,128)S(1)} copy-done((f32[8,8,128]{2,1,0:T(8,128)S(1)}, f32[8,8,128]{2,1,0:T(8,128)}, u32[]{:S(2)}) %copy-start.1) | copy-done | bytes 32792
  2.2 0.0 copy-start.3
  2.2 0.7 %copy-done.3 = s32[1,1,1,3,4,8]{5,4,3,2,1,0:T(4,128)S(1)} copy-done((s32[1,1,1,3,4,8]{5,4,3,2,1,0:T(4,128)S(1)}, s32[1,1,1,3,4,8]{5,4,3,2,1,0:T(4,128)}, u32[]{:S(2)}) %copy-start.3) | copy-done | bytes 408
  2.9 0.0 copy-start.5
  2.9 0.7 %copy-done.5 = f32[1,1,1,4,8]{4,3,2,1,0:T(4,128)S(1)} copy-done((f32[1,1,1,4,8]{4,3,2,1,0:T(4,128)S(1)}, f32[1,1,1,4,8]{4,3,2,1,0:T(4,128)}, u32[]{:S(2)}) %copy-start.5) | copy-done | bytes 152
  3.6 19.5 %shard_map.73 = f32[8,8,128]{2,1,0:T(8,128)S(1)} custom-call(f32[8,8,128]{2,1,0:T(8,128)S(1)} %copy-done, f32[8,8,128]{2,1,0:T(8,128)S(1)} %copy-done.1, f32[3,4,8]{2,1,0:T(4,128)S(1)} %bitcast.5, f32[4,8]{1,0:T(4,128)S(1)} %bitcast.7, f32[4,8]{1,0:T(4,128)S(1)} %bitcast.8, s32[1,4]{1,0:T(1,128)S(1)} %bitcast.9, s32[3,4,8]{2,1,0:T(4,128)S(1)} %bitcast.6), custom_call_target="tpu_custom_call" | custom-call | tf_op jit(solution)/shard_map/pallas_call | solution.py:351
  23.1 0.6 %copy.9 = f32[8,8,128]{2,1,0:T(8,128)} copy(f32[8,8,128]{2,1,0:T(8,128)S(1)} %shard_map.73) | data formatting | bytes 65536
Async XLA Ops:
  0.0 0.7 %copy-start.2 = (f32[1,1,1,3,4,8]{5,4,3,2,1,0:T(4,128)S(1)}, f32[1,1,1,3,4,8]{5,4,3,2,1,0:T(4,128)}, u32[]{:S(2)}) copy-start(f32[1,1,1,3,4,8]{5,4,3,2,1,0:T(4,128)} %param.9) | copy-start | bytes 1156
  0.0 0.7 %copy-start.4 = (f32[1,1,1,4,8]{4,3,2,1,0:T(4,128)S(1)}, f32[1,1,1,4,8]{4,3,2,1,0:T(4,128)}, u32[]{:S(2)}) copy-start(f32[1,1,1,4,8]{4,3,2,1,0:T(4,128)} %param.10) | copy-start | bytes 388
  0.0 0.7 %copy-start.6 = (s32[1,1,1,4]{3,2,1,0:T(1,128)S(1)}, s32[1,1,1,4]{3,2,1,0:T(1,128)}, u32[]{:S(2)}) copy-start(s32[1,1,1,4]{3,2,1,0:T(1,128)} %param.12) | copy-start | bytes 52
  0.7 0.8 %copy-start = (f32[8,8,128]{2,1,0:T(8,128)S(1)}, f32[8,8,128]{2,1,0:T(8,128)}, u32[]{:S(2)}) copy-start(f32[8,8,128]{2,1,0:T(8,128)} %charge_ref.1) | copy-start | bytes 98308
  1.5 0.8 %copy-start.1 = (f32[8,8,128]{2,1,0:T(8,128)S(1)}, f32[8,8,128]{2,1,0:T(8,128)}, u32[]{:S(2)}) copy-start(f32[8,8,128]{2,1,0:T(8,128)} %eps_ref.1) | copy-start | bytes 98308
  2.2 0.7 %copy-start.3 = (s32[1,1,1,3,4,8]{5,4,3,2,1,0:T(4,128)S(1)}, s32[1,1,1,3,4,8]{5,4,3,2,1,0:T(4,128)}, u32[]{:S(2)}) copy-start(s32[1,1,1,3,4,8]{5,4,3,2,1,0:T(4,128)} %param.13) | copy-start | bytes 1156
  2.9 0.7 %copy-start.5 = (f32[1,1,1,4,8]{4,3,2,1,0:T(4,128)S(1)}, f32[1,1,1,4,8]{4,3,2,1,0:T(4,128)}, u32[]{:S(2)}) copy-start(f32[1,1,1,4,8]{4,3,2,1,0:T(4,128)} %param.11) | copy-start | bytes 388

commit v2 on v1

--- a/solution.py
+++ b/solution.py
@@ -55,6 +55,20 @@
     if step > 0:
         return jnp.concatenate([values[1:], zero], 0)
     return jnp.concatenate([zero, values[:-1]], 0)
+
+
+def packed(values):
+    a, b, c = values.shape
+    v = values.reshape(a // 2, 2, b, c)
+    return jnp.where(iota((a // 2, b, c), 2) % 2 == 0, v[:, 0], v[:, 1])
+
+
+def unpacked(values):
+    a, b, c = values.shape
+    even = iota(values.shape, 2) % 2 == 0
+    first = jnp.where(even, values, rolled(values, 1, 2))
+    second = jnp.where(even, rolled(values, -1, 2), values)
+    return jnp.stack([first, second], 1).reshape(2 * a, b, c)
 
 
 class Coarse:
@@ -108,14 +122,15 @@
 
 def kernel(
     sizes,
-    charge_ref, eps_ref, centers_ref, widths_ref, charges_ref, counts_ref, anchors_ref,
+    charge_in, eps_in, centers_in, widths_in, charges_in, counts_in, anchors_in,
     out_ref,
+    charge_ref, eps_ref, centers_ref, widths_ref, charges_ref, counts_ref, anchors_ref, load_sem,
     f_ref, hx_ref, hy_ref, hz_ref, sy_ref, pairs_ref, gather_ref, ions_out, ions_in, whole1, half2, up1, up0,
     face_send, face_recv, gather_send, gather_recv, ion_send, ion_recv,
 ):
     ngx, ngy, ngz = sizes
     cx, cy, cz = charge_ref.shape
-    bx, by = cx // 2, cy // 2
+    bx, by, hx = cx // 2, cy // 2, cx // 4
     n = ngx * ngy * ngz
     gx, gy, gz = lax.axis_index("gx"), lax.axis_index("gy"), lax.axis_index("gz")
     me = (gx * ngy + gy) * ngz + gz
@@ -124,6 +139,14 @@
         at = (me + k) % n
         return {"gx": at // (ngy * ngz), "gy": (at // ngz) % ngy, "gz": at % ngz}
 
+    loads = [
+        pltpu.make_async_copy(source, target, load_sem.at[index])
+        for index, (source, target) in enumerate((
+            (eps_in, eps_ref), (counts_in, counts_ref), (centers_in, centers_ref), (widths_in, widths_ref),
+            (charges_in, charges_ref), (anchors_in, anchors_ref), (charge_in, charge_ref)))
+    ]
+    for load in loads:
+        load.start()
     barrier = pltpu.get_barrier_semaphore()
     each(n, lambda k: pl.semaphore_signal(barrier, inc=1, device_id=peer(k), device_id_type=MESH))
 
@@ -197,12 +220,16 @@
         for a in range(ngx):
             for b in range(ngy):
                 for c in range(ngz):
-                    whole1[a * bx : (a + 1) * bx, b * by : (b + 1) * by, c * cz : (c + 1) * cz] = gather_ref[
+                    whole1[a * hx : (a + 1) * hx, b * by : (b + 1) * by, c * cz : (c + 1) * cz] = gather_ref[
                         kind, (a * ngy + b) * ngz + c]
-        return whole1[...]
-
+        return unpacked(whole1[...])
+
+    up0[...] = jnp.zeros_like(up0)
+    loads[0].wait()
     eps = eps_ref[...]
-    gather_ref[0, me] = restrict(eps)
+    gather_ref[0, me] = packed(restrict(eps))
+    for load in loads[1:6]:
+        load.wait()
     counts = counts_ref[...]
     for d in range(ngy):
         for c in range(3):
@@ -214,7 +241,6 @@
         ions_out[d, 6:8, 0:CAP] = jnp.zeros((2, CAP), jnp.float32)
         ions_out[d, :, CAP:] = jnp.ones((8, 128 - CAP), jnp.float32)
     ions_in[gy] = ions_out[gy]
-    up0[...] = jnp.zeros_like(up0)
 
     pl.semaphore_wait(barrier, n - 1)
     each(ngy, lambda k: ion_copy(k).start())
@@ -242,6 +268,7 @@
             density += block.astype(jnp.bfloat16).astype(jnp.float32)
         return density
 
+    loads[6].wait()
     density = charge_ref[...]
     if ngy <= 4:
         for source in range(ngy):
@@ -264,7 +291,7 @@
     send_faces(1, f_ref)
 
     each(n, lambda k: gather_copy(0, k).wait_recv())
-    nx1, ny1 = whole1.shape[:2]
+    nx1, ny1 = 2 * whole1.shape[0], whole1.shape[1]
 
     def down_y(values):
         rows = ny1 // 2
@@ -298,7 +325,7 @@
         return total
 
     f_halo = halo(1)
-    gather_ref[1, me] = restrict((1.0 / 3.0) * g + beside(f, f_halo))
+    gather_ref[1, me] = packed(restrict((1.0 / 3.0) * g + beside(f, f_halo)))
     each(n, lambda k: gather_copy(1, k).start())
     each(n, lambda k: gather_copy(1, k).wait_recv())
 
@@ -350,27 +377,35 @@
         dma = pltpu.SemaphoreType.DMA
         return pl.pallas_call(
             functools.partial(kernel, (ngx, ngy, ngz)),
-            out_shape=jax.ShapeDtypeStruct((cx, cy, cz), f32),
-            in_specs=[pl.BlockSpec(memory_space=pltpu.VMEM)] * 7,
+            out_shape=pltpu.VMEM((cx, cy, cz), f32),
+            in_specs=[pl.BlockSpec(memory_space=pltpu.HBM)] * 7,
             out_specs=pl.BlockSpec(memory_space=pltpu.VMEM),
             scratch_shapes=[
+                pltpu.VMEM((cx, cy, cz), f32),
+                pltpu.VMEM((cx, cy, cz), f32),
+                pltpu.VMEM((3, ngy, CAP), f32),
+                pltpu.VMEM((ngy, CAP), f32),
+                pltpu.VMEM((ngy, CAP), f32),
+                pltpu.VMEM((1, ngy), jnp.int32),
+                pltpu.VMEM((3, ngy, CAP), jnp.int32),
+                dma((7,)),
                 pltpu.VMEM((cx, cy, cz), f32),
                 pltpu.VMEM((2, 2, cy, cz), f32),
                 pltpu.VMEM((2, 2, cx, 1, cz), f32),
                 pltpu.VMEM((2, 2, cx, cy, cz), f32),
                 pltpu.VMEM((2, 2, cx, 1, cz), f32),
                 pltpu.VMEM((cx // 2, cy, cz), f32),
-                pltpu.VMEM((2, n, cx // 2, cy // 2, cz), f32),
+                pltpu.VMEM((2, n, cx // 4, cy // 2, cz), f32),
                 pltpu.VMEM((ngy, 8, 128), f32),
                 pltpu.VMEM((ngy, 8, 128), f32),
-                pltpu.VMEM((nx1, ny1, ngz * cz), f32),
+                pltpu.VMEM((nx1 // 2, ny1, ngz * cz), f32),
                 pltpu.VMEM((ngz, nx1 // 2, ny1, cz), f32),
                 pltpu.VMEM((ngz, nx1, ny1, cz), f32),
                 pltpu.VMEM((ngz + 2, nx1 + 2, (ngy + 2) * cy, cz), f32),
                 dma((12,)), dma((12,)), dma((2, n)), dma((2, n)), dma((ngy,)), dma((ngy,)),
             ],
             compiler_params=pltpu.CompilerParams(
-                collective_id=0, has_side_effects=True, vmem_limit_bytes=48 * 1024 * 1024),
+                collective_id=0, has_side_effects=True, vmem_limit_bytes=65408 * 1024),
         )(
             charge_density,
             permittivity,

time: 24.1 us -> 20.3 us (0.84)
  local copies, waits for them, and re-layouts: 4.2 us -> 0.62 us
    unnamed x15 -> x1, local copies, waits for them, and re-layouts: 4.2 us -> 0.62 us
where the time goes in v2:
time: 20.3 us; the launch traced here: 20.1 us
  Pallas kernels  19.5 us (96%)
  local copies, waits for them, and re-layouts  0.62 us (3%)
    pallas_call x1, Pallas kernels, per_device(): pl.pallas_call(functools.partial(kernel, (ngx, ngy, ngz)), out_shape=pltp...  19.5 us
    unnamed x1, local copies, waits for them, and re-layouts  0.62 us

profile of v2, /device:TPU:0, one launch (start us, length us, event | category | flops | bytes accessed | tf_op | source)
XLA Modules:
  0.0 20.1 jit_solution(16189104821678412596)
XLA Ops:
  0.0 19.5 %shard_map.73 = f32[8,8,128]{2,1,0:T(8,128)S(1)} custom-call(f32[8,8,128]{2,1,0:T(8,128)} %charge_in.1, f32[8,8,128]{2,1,0:T(8,128)} %eps_in.1, f32[3,4,8]{2,1,0:T(4,128)} %bitcast.5, f32[4,8]{1,0:T(4,128)} %bitcast.7, f32[4,8]{1,0:T(4,128)} %bitcast.8, s32[1,4]{1,0:T(1,128)} %bitcast.9, s32[3,4,8]{2,1,0:T(4,128)} %bitcast.6), custom_call_target="tpu_custom_call" | custom-call | tf_op jit(solution)/shard_map/pallas_call | solution.py:378
  19.5 0.6 %copy.9 = f32[8,8,128]{2,1,0:T(8,128)} copy(f32[8,8,128]{2,1,0:T(8,128)S(1)} %shard_map.73) | data formatting | bytes 65536

commit v3 on v2

--- a/solution.py
+++ b/solution.py
@@ -202,8 +202,12 @@
     def gather_copy(kind, k):
         return pltpu.make_async_remote_copy(
             src_ref=gather_ref.at[kind, me], dst_ref=gather_ref.at[kind, me],
-            send_sem=gather_send.at[kind, k], recv_sem=gather_recv.at[kind, k],
+            send_sem=gather_send.at[kind], recv_sem=gather_recv.at[kind],
             device_id=peer(k), device_id_type=MESH)
+
+    def wait_gather(kind, semaphore):
+        blocks = gather_ref.at[kind, pl.ds(0, n - 1)]
+        pltpu.make_async_copy(blocks, blocks, semaphore.at[kind]).wait()
 
     def ion_copy(k):
         to = (gy + k) % ngy
@@ -290,7 +294,7 @@
     f_ref[...] = f
     send_faces(1, f_ref)
 
-    each(n, lambda k: gather_copy(0, k).wait_recv())
+    wait_gather(0, gather_recv)
     nx1, ny1 = 2 * whole1.shape[0], whole1.shape[1]
 
     def down_y(values):
@@ -327,7 +331,12 @@
     f_halo = halo(1)
     gather_ref[1, me] = packed(restrict((1.0 / 3.0) * g + beside(f, f_halo)))
     each(n, lambda k: gather_copy(1, k).start())
-    each(n, lambda k: gather_copy(1, k).wait_recv())
+    each(ngy, lambda k: ion_copy(k).wait_send())
+    wait_faces(0, eps_ref, True)
+    wait_faces(1, f_ref, True)
+    wait_gather(0, gather_send)
+    wait_gather(1, gather_send)
+    wait_gather(1, gather_recv)
 
     g1 = assemble(1)
     f1 = level1.first(g1)
@@ -358,12 +367,6 @@
         (zl + repeat_x(part(1, bx, 1, 0)), zh + repeat_x(part(1, bx, 1, 2))),
     )
     out_ref[...] = (1.0 / 3.0) * f + inverse * (g + beside(f, f_halo))
-
-    each(ngy, lambda k: ion_copy(k).wait_send())
-    wait_faces(0, eps_ref, True)
-    wait_faces(1, f_ref, True)
-    each(n, lambda k: gather_copy(0, k).wait_send())
-    each(n, lambda k: gather_copy(1, k).wait_send())
 
 
 def solution(mesh):
@@ -402,7 +405,7 @@
                 pltpu.VMEM((ngz, nx1 // 2, ny1, cz), f32),
                 pltpu.VMEM((ngz, nx1, ny1, cz), f32),
                 pltpu.VMEM((ngz + 2, nx1 + 2, (ngy + 2) * cy, cz), f32),
-                dma((12,)), dma((12,)), dma((2, n)), dma((2, n)), dma((ngy,)), dma((ngy,)),
+                dma((12,)), dma((12,)), dma((2,)), dma((2,)), dma((ngy,)), dma((ngy,)),
             ],
             compiler_params=pltpu.CompilerParams(
                 collective_id=0, has_side_effects=True, vmem_limit_bytes=65408 * 1024),

time: 20.3 us -> 19.7 us (0.970)
  Pallas kernels: 19.5 us -> 18.9 us
    pallas_call x1, Pallas kernels: 19.5 us -> 18.9 us  [per_device(): pl.pallas_call(functools.partial(kernel, (ngx, ngy, ngz)), out_shape=pltp...]
where the time goes in v3:
time: 19.7 us; the launch traced here: 19.5 us
  Pallas kernels  18.9 us (96%)
  local copies, waits for them, and re-layouts  0.62 us (3%)
    pallas_call x1, Pallas kernels, per_device(): pl.pallas_call(functools.partial(kernel, (ngx, ngy, ngz)), out_shape=pltp...  18.9 us
    unnamed x1, local copies, waits for them, and re-layouts  0.62 us

profile of v3, /device:TPU:0, one launch (start us, length us, event | category | flops | bytes accessed | tf_op | source)
XLA Modules:
  0.0 19.5 jit_solution(14301922783722149462)
XLA Ops:
  0.0 18.9 %shard_map.73 = f32[8,8,128]{2,1,0:T(8,128)S(1)} custom-call(f32[8,8,128]{2,1,0:T(8,128)} %charge_in.1, f32[8,8,128]{2,1,0:T(8,128)} %eps_in.1, f32[3,4,8]{2,1,0:T(4,128)} %bitcast.5, f32[4,8]{1,0:T(4,128)} %bitcast.7, f32[4,8]{1,0:T(4,128)} %bitcast.8, s32[1,4]{1,0:T(1,128)} %bitcast.9, s32[3,4,8]{2,1,0:T(4,128)} %bitcast.6), custom_call_target="tpu_custom_call" | custom-call | tf_op jit(solution)/shard_map/pallas_call | solution.py:381
  18.9 0.6 %copy.9 = f32[8,8,128]{2,1,0:T(8,128)} copy(f32[8,8,128]{2,1,0:T(8,128)S(1)} %shard_map.73) | data formatting | bytes 65536
